TPU v7x, 32 devices: a whole 2x2x4 slice. The times are simulated.
32 devices in a mesh: groups: 2 (over y), tp: 4 (over z), sp: 2 (over x), ep: 2 (over core).
Axes of the slice: x: 2, y: 2, z: 4, core: 2. Of those that a mesh axis runs over, the one named last changes fastest.
Arguments:
- activations: bfloat16 [4096, 8192], P(('groups', 'sp'), 'tp'), parts along dimension 0, may hold values from -6 to 6
- output_projection_weight: bfloat16 [8192, 8192], P('tp'), may hold values from -0.09375 to 0.09375
- shrink_matrices: bfloat16 [32, 8192, 64], P(('sp', 'ep'), 'tp'), may hold values from -0.0625 to 0.0625
- expand_matrices: bfloat16 [32, 64, 8192], P(('sp', 'ep'), None, 'tp'), may hold values from -0.75 to 0.75
- tenant_of_block: int32 [32], P(('groups', 'sp')), parts along dimension 0, may hold values from 0 to 31
- token_rows_per_block: int32 [32], P(('groups', 'sp')), parts along dimension 0, may hold values from 1 to 128, as said below
- tenant_table_row: int32 [32], replicated, may hold values from 0 to 31, each once
Outputs:
- projected: bfloat16 [4096, 8192], P(('groups', 'sp'), 'tp'), parts along dimension 0
There are 2 independent parts, one for each index of `groups`. A program takes and returns all parts, laid end to end along the dimension named above; an argument that names none is the same for every part. Nothing has to cross between parts.
Inputs may be any that keep to these rules, and one draw needn't show every extreme that they name: `token_rows_per_block`: each index of sp holds at least one block with all 128 rows live. `tenant_table_row`: each tenant id appears once.
All inputs are finite; a program needn't handle non-finite values.
Results may differ from a plain program's by a relative error of at most 0.012.
Values may be sent and summed in bfloat16 or wider, within the bound.
A program may use at most 192 MiB of HBM per device.

v0:
```python
import jax
import jax.numpy as jnp
from jax import lax
from jax.sharding import PartitionSpec as P

BLOCK = 128


def per_device(
    activations,
    output_projection_weight,
    shrink_matrices,
    expand_matrices,
    tenant_of_block,
    token_rows_per_block,
    tenant_table_row,
):
    width = activations.shape[1]
    blocked = activations.reshape(-1, BLOCK, width)
    tenant_ids = jnp.arange(tenant_table_row.shape[0], dtype=jnp.int32)
    tenant_onehot = (tenant_of_block[:, None] == tenant_ids[None, :]).astype(jnp.int32)
    block_table_rows = jnp.sum(tenant_onehot * tenant_table_row[None, :], axis=1)

    def gather_table_rows(table_piece):
        local_ids = jnp.arange(table_piece.shape[0], dtype=jnp.int32)
        chosen = (block_table_rows[:, None] == local_ids[None, :]).astype(table_piece.dtype)
        return jnp.einsum("bj,jkl->bkl", chosen, table_piece, preferred_element_type=jnp.float32)

    picked_adapters = gather_table_rows(
        lax.all_gather(shrink_matrices, ("sp", "ep"), axis=0, tiled=True)
    ).astype(jnp.bfloat16)
    shrink_part = jnp.einsum(
        "bnd,bdr->bnr", blocked, picked_adapters, preferred_element_type=jnp.float32
    )
    chosen_up_matrix = gather_table_rows(
        lax.all_gather(expand_matrices, ("sp", "ep"), axis=0, tiled=True)
    )
    shrink = lax.psum(shrink_part.astype(jnp.bfloat16), "tp").astype(jnp.float32)
    row_index = jnp.arange(BLOCK, dtype=jnp.int32)
    live = row_index[None, :] < token_rows_per_block[:, None]
    shrink = jnp.where(live[:, :, None], shrink, jnp.zeros_like(shrink)).astype(jnp.bfloat16)
    delta = jnp.einsum(
        "bnr,brd->bnd",
        shrink,
        chosen_up_matrix.astype(jnp.bfloat16),
        preferred_element_type=jnp.float32,
    )
    delta = delta.reshape(-1, width)
    partial_term = jnp.dot(
        activations, output_projection_weight, preferred_element_type=jnp.float32
    )
    base = lax.psum_scatter(
        partial_term.astype(jnp.bfloat16), "tp", scatter_dimension=1, tiled=True
    ).astype(jnp.float32)
    return (base + delta).astype(jnp.bfloat16)


def solution(mesh):
    in_specs = (
        P(("groups", "sp"), "tp"),
        P("tp", None),
        P(("sp", "ep"), "tp", None),
        P(("sp", "ep"), None, "tp"),
        P(("groups", "sp")),
        P(("groups", "sp")),
        P(),
    )
    out_specs = P(("groups", "sp"), "tp")
    return jax.shard_map(
        per_device, mesh=mesh, in_specs=in_specs, out_specs=out_specs, check_vma=False
    )
```

profile of v0, /device:TPU:17, one launch (start us, length us, event | category | flops | bytes accessed | tf_op | source)
XLA Modules:
  0.0 462.9 jit_solution(4760983154785489442)
XLA Ops:
  6.5 0.0 copy-start.1
  6.5 0.0 copy-start.2
  6.5 0.0 all-gather.3.cloned.1.call-start
  6.5 0.7 all-gather.3.cloned.1.call-update
  7.3 0.0 all-gather.5.cloned.1.call-start
  7.3 0.7 all-gather.5.cloned.1.call-update
  8.0 0.0 all-reduce.2.cloned.1.call-start
  8.1 0.0 copy-done.1
  8.1 0.0 copy-done.2
  8.1 0.2 select_reduce_fusion
  8.3 60.5 %all-gather.3.cloned.1.call-done = bf16[32,2048,64]{1,2,0:T(8,128)(2,1)} async-done(((bf16[8,2048,64]{1,2,0:T(8,128)(2,1)}), bf16[32,2048,64]{1,2,0:T(8,128)(2,1)}) %all-gather.3.cloned.1.call-update) | async-done | bytes 8388624 | tf_op jit(solution)/shard_map/all_gather | solution.py:30
  68.7 0.0 copy-start
  68.7 12.5 %fusion.5 = bf16[8,2048,64]{1,0,2:T(8,128)(2,1)S(1)} fusion(bf16[32,2048,64]{1,2,0:T(8,128)(2,1)} %all-gather.3.cloned.1.call-done, s32[8]{0:T(128)S(1)} %select_reduce_fusion), kind=kOutput, calls=%fused_computation.7 | convolution fusion | flops 68157696 | bytes 10485792 | tf_op jit(solution)/shard_map/bj,jkl->bkl/dot_general | solution.py:27
  81.2 0.0 copy-done
  81.2 2.4 fusion.18
  83.6 0.0 all-reduce.2.cloned.1.call-update
  83.6 0.2 reduce-scatter.2.cloned.1.call-start
  83.9 41.8 %convolution_convert_fusion = bf16[1024,8192]{1,0:T(8,128)(2,1)} fusion(bf16[1024,2048]{1,0:T(8,128)(2,1)} %param.7, bf16[2048,8192]{1,0:T(8,128)(2,1)} %param.8), kind=kOutput, calls=%fused_computation | convolution fusion | flops 34368126976 | bytes 54525952 | tf_op jit(solution)/shard_map/dot_general | solution.py:49
  125.7 0.0 copy-start.3
  125.7 0.0 reduce-scatter.2.cloned.1.call-update
  125.7 0.6 copy-done.3
  126.4 0.1 iota_compare_fusion.2
  126.4 2.2 all-gather.5.cloned.1.call-done
  128.6 12.3 %fusion.8 = bf16[8,64,2048]{2,0,1:T(8,128)(2,1)S(1)} fusion(bf16[32,64,2048]{2,1,0:T(8,128)(2,1)} %all-gather.5.cloned.1.call-done, s32[8]{0:T(128)S(1)} %select_reduce_fusion), kind=kOutput, calls=%fused_computation.8 | convolution fusion | flops 68157696 | bytes 10485792 | tf_op jit(solution)/shard_map/bj,jkl->bkl/dot_general | solution.py:27
  140.9 21.7 %all-reduce.2.cloned.1.call-done = bf16[8,128,64]{1,2,0:T(8,128)(2,1)} async-done(((bf16[8,128,64]{1,2,0:T(8,128)(2,1)}), bf16[8,128,64]{1,2,0:T(8,128)(2,1)}) %all-reduce.2.cloned.1.call-update) | async-done | bytes 131088 | tf_op jit(solution)/shard_map/psum | solution.py:38
  162.7 7.3 %fusion.11 = f32[8,128,2048]{2,1,0:T(8,128)} fusion(bf16[8,64,2048]{2,0,1:T(8,128)(2,1)S(1)} %fusion.8, bf16[8,128,64]{1,2,0:T(8,128)(2,1)} %all-reduce.2.cloned.1.call-done, pred[8,128]{1,0:T(8,128)(4,1)S(1)} %iota_compare_fusion.2), kind=kOutput, calls=%fused_computation.9 | convolution fusion | flops 268632064 | bytes 10617856 | tf_op jit(solution)/shard_map/bnr,brd->bnd/dot_general | solution.py:42
  170.0 278.1 %reduce-scatter.2.cloned.1.call-done = bf16[1024,2048]{1,0:T(8,128)(2,1)} async-done(((bf16[1024,8192]{1,0:T(8,128)(2,1)}), bf16[1024,2048]{1,0:T(8,128)(2,1)}) %reduce-scatter.2.cloned.1.call-update) | async-done | bytes 4194320 | tf_op jit(solution)/shard_map/reduce_scatter | solution.py:52
  448.1 8.3 %fusion = bf16[1024,2048]{1,0:T(8,128)(2,1)} fusion(f32[8,128,2048]{2,1,0:T(8,128)} %fusion.11, bf16[1024,2048]{1,0:T(8,128)(2,1)} %reduce-scatter.2.cloned.1.call-done), kind=kLoop, calls=%fused_computation.2 | loop fusion | flops 6291456 | bytes 16777216 | tf_op jit(solution)/shard_map/convert_element_type | solution.py:55
Async XLA Ops:
  6.5 1.5 copy-start.1
  6.5 1.5 copy-start.2
  6.5 62.2 %all-gather.3.cloned.1.call-start = ((), (), s32[]{:S(2)}) async-start(), calls=%async_computation.2 | async-start | bytes 10485760 | tf_op jit(solution)/shard_map/all_gather | solution.py:30
  7.3 121.4 %all-gather.5.cloned.1.call-start = ((), (), s32[]{:S(2)}) async-start(), calls=%async_computation.4 | async-start | bytes 10485760 | tf_op jit(solution)/shard_map/all_gather | solution.py:36
  8.0 154.7 %all-reduce.2.cloned.1.call-start = ((), (), s32[]{:S(2)}) async-start(), calls=%async_computation.3 | async-start | bytes 262144 | tf_op jit(solution)/shard_map/psum | solution.py:38
  68.7 12.5 %copy-start = (bf16[1024,2048]{1,0:T(8,128)(2,1)S(1)}, bf16[1024,2048]{1,0:T(8,128)(2,1)}, u32[]{:S(2)}) copy-start(bf16[1024,2048]{1,0:T(8,128)(2,1)} %param.7) | copy-start | bytes 12582916
  83.6 364.5 %reduce-scatter.2.cloned.1.call-start = ((), (), s32[]{:S(2)}) async-start(), calls=%async_computation.1 | async-start | bytes 20971520 | tf_op jit(solution)/shard_map/reduce_scatter | solution.py:52
  125.7 0.7 copy-start.3
Sparse Core Ops, SparseCore 0:
  8.9 59.7 all-gather.2
  70.3 58.2 all-gather.4
  130.9 31.6 all-reduce.1
  165.0 283.0 reduce-scatter.1
where the time goes:
time: 464 us; the launch traced here: 463 us
  waiting for transfers between devices  364 us (78%)
  matrix products  76.3 us (16%)
  between operations  13.1 us (3%)
  other arithmetic  8.54 us (2%)
    reduce_scatter x1, waiting for transfers between devices, per_device(): lax.psum_scatter(partial_term.astype(jnp.bfloat16), 'tp', scatter_dimensi...  278 us
    all_gather x1, waiting for transfers between devices, per_device(): lax.all_gather(shrink_matrices, ('sp', 'ep'), axis=0, tiled=True)  60.5 us
    dot_general x1, matrix products, per_device(): jnp.dot(activations, output_projection_weight, preferred_element_type=jnp...  41.8 us
    dot_general x2, matrix products, gather_table_rows(): jnp.einsum('bj,jkl->bkl', chosen, table_piece, preferred_element_type=jnp...  24.8 us
    psum x1, waiting for transfers between devices, per_device(): lax.psum(shrink_part.astype(jnp.bfloat16), 'tp').astype(jnp.float32)  21.7 us
  transfers between devices with their start and end apart: 4, of which 4 were waited for; matrix products, arithmetic and copies ran while one was open for 17% of the time, Pallas kernels for 0%

commit v1 on v0

v1 whole, which is shorter than its diff:
```python
import functools

import jax
import jax.numpy as jnp
from jax import lax
from jax.experimental import pallas as pl
from jax.experimental.pallas import tpu as pltpu
from jax.sharding import PartitionSpec as P

BLOCK = 128
CHUNK = 512
MESH = pl.DeviceIdType.MESH
F32 = jnp.float32
BF16 = jnp.bfloat16


def kernel(
    n,
    n_sp,
    n_ep,
    chunk,
    tenant_ref,
    live_ref,
    table_ref,
    x_hbm,
    w_hbm,
    a_hbm,
    b_hbm,
    o_hbm,
    x_v,
    w_v,
    prod,
    right,
    left,
    own,
    out_v,
    a_all,
    b_all,
    packs,
    lhs,
    x_sem,
    w_sem,
    right_send,
    right_recv,
    left_send,
    left_recv,
    a_local,
    a_send,
    a_recv,
    b_local,
    b_send,
    b_recv,
    pack_send,
    pack_recv,
    out_local,
    out_send,
    out_recv,
):
    z = lax.axis_index("tp")
    s = lax.axis_index("sp")
    e = lax.axis_index("ep")
    rows, depth = x_v.shape
    half = depth // 2
    width = o_hbm.shape[1]
    per = width // chunk
    blocks = rows // BLOCK
    pieces = a_hbm.shape[0]
    moving = (n - 1) * per
    row0 = pl.multiple_of(e * rows, BLOCK)

    x_copy = pltpu.make_async_copy(x_hbm.at[pl.ds(row0, rows), :], x_v, x_sem)
    x_copy.start()

    n_right = (n - 1 - z) * per
    n_left = z * per
    in_low = z < n // 2
    n_first = jnp.where(in_low, n_right, n_left)
    n_second = moving - n_first

    def item(i):
        paired = i <= 2 * n_second
        odd = i % 2
        index = jnp.where(
            paired,
            jnp.where(odd == 1, (i + 1) // 2, jnp.where(i == 0, 0, i // 2 - 1)),
            i - n_second,
        )
        second = jnp.where(paired & (odd == 0) & (i > 0), 1, 0)
        is_own = i >= moving
        goes_right = jnp.where(in_low, 1 - second, second)
        kind = jnp.where(is_own, 2, jnp.where(goes_right == 1, 0, 1))
        index = jnp.where(is_own, i - moving, index)
        return kind, index

    def column_of(i):
        kind, index = item(i)
        steps = index // per
        dest = jnp.where(kind == 2, z, jnp.where(kind == 0, n - 1 - steps, steps))
        return pl.multiple_of(dest * width + (index % per) * chunk, chunk)

    def w_copy(i):
        slot = i % 2
        return pltpu.make_async_copy(
            w_hbm.at[:, pl.ds(column_of(i), chunk)], w_v.at[slot], w_sem.at[slot]
        )

    w_copy(0).start()

    barrier = pltpu.get_barrier_semaphore()
    for k in range(1, n):
        pl.semaphore_signal(
            barrier, inc=1, device_id={"tp": lax.rem(z + k, n)}, device_id_type=MESH
        )
    for k in range(1, n_sp):
        pl.semaphore_signal(
            barrier, inc=1, device_id={"sp": lax.rem(s + k, n_sp)}, device_id_type=MESH
        )
    for k in range(1, n_ep):
        pl.semaphore_signal(
            barrier, inc=1, device_id={"ep": lax.rem(e + k, n_ep)}, device_id_type=MESH
        )
    pl.semaphore_wait(barrier, n + n_sp + n_ep - 3)

    sibling = {"ep": lax.rem(e + 1, n_ep)}

    def part(ref, owner_s, owner_e):
        start = (owner_s * n_ep + owner_e) * pieces
        return ref.at[pl.ds(start, pieces)]

    def along_sp(src, gathered, send, recv, k):
        return pltpu.make_async_remote_copy(
            src_ref=src,
            dst_ref=part(gathered, s, e),
            send_sem=send.at[k],
            recv_sem=recv.at[k],
            device_id={"sp": lax.rem(s + k, n_sp)},
            device_id_type=MESH,
        )

    def along_ep(src, gathered, send, recv, k):
        return pltpu.make_async_remote_copy(
            src_ref=src,
            dst_ref=part(gathered, lax.rem(s + n_sp - k, n_sp), e),
            send_sem=send.at[n_sp + k],
            recv_sem=recv.at[n_sp + k],
            device_id=sibling,
            device_id_type=MESH,
        )

    tables = (
        (a_hbm, a_all, a_local, a_send, a_recv),
        (b_hbm, b_all, b_local, b_send, b_recv),
    )

    def start_table(src, gathered, local, send, recv):
        for k in range(1, n_sp):
            along_sp(src, gathered, send, recv, k).start()
        along_ep(src, gathered, send, recv, 0).start()
        pltpu.make_async_copy(src, part(gathered, s, e), local).start()

    def forward_table(src, gathered, local, send, recv):
        for k in range(1, n_sp):
            along_sp(src, gathered, send, recv, k).wait_recv()
            piece = part(gathered, lax.rem(s + n_sp - k, n_sp), e)
            along_ep(piece, gathered, send, recv, k).start()

    def finish_table(src, gathered, local, send, recv):
        pltpu.make_async_copy(src, part(gathered, s, e), local).wait()
        for k in range(n_sp):
            along_ep(src, gathered, send, recv, k).wait_recv()

    def drain_table(src, gathered, local, send, recv):
        for k in range(1, n_sp):
            along_sp(src, gathered, send, recv, k).wait_send()
        for k in range(n_sp):
            along_ep(src, gathered, send, recv, k).wait_send()

    def right_copy(t):
        return pltpu.make_async_remote_copy(
            src_ref=right.at[t],
            dst_ref=right.at[t],
            send_sem=right_send.at[t],
            recv_sem=right_recv.at[t],
            device_id={"tp": z + 1},
            device_id_type=MESH,
        )

    def left_copy(t):
        return pltpu.make_async_remote_copy(
            src_ref=left.at[t],
            dst_ref=left.at[t],
            send_sem=left_send.at[t],
            recv_sem=left_recv.at[t],
            device_id={"tp": z - 1},
            device_id_type=MESH,
        )

    def step(i, carry):
        kind, t = item(i)
        slot = i % 2

        @pl.when(i + 1 < n * per)
        def _():
            w_copy(i + 1).start()

        w_copy(i).wait()
        prod[...] = jnp.dot(x_v[...], w_v[slot], preferred_element_type=F32)

        @pl.when(kind == 0)
        def _():
            @pl.when(z > 0)
            def _():
                right_copy(t).wait_recv()
                right[t] = (prod[...] + right[t].astype(F32)).astype(BF16)

            @pl.when(z == 0)
            def _():
                right[t] = prod[...].astype(BF16)

            right_copy(t).start()

        @pl.when(kind == 1)
        def _():
            @pl.when(z < n - 1)
            def _():
                left_copy(t).wait_recv()
                left[t] = (prod[...] + left[t].astype(F32)).astype(BF16)

            @pl.when(z == n - 1)
            def _():
                left[t] = prod[...].astype(BF16)

            left_copy(t).start()

        @pl.when(kind == 2)
        def _():
            own[t] = prod[...]

        return carry

    start_table(*tables[0])
    x_copy.wait()
    step(0, 0)
    start_table(*tables[1])
    turn_a = min(5, moving)
    turn_b = min(7, moving)
    lax.fori_loop(1, turn_a, step, 0)
    forward_table(*tables[0])
    lax.fori_loop(turn_a, turn_b, step, 0)
    finish_table(*tables[0])

    lane = lax.broadcasted_iota(jnp.int32, (BLOCK, 128), 1)
    rank = lane.shape[1] // 2

    def shrink_pair(b):
        slot = table_ref[tenant_ref[e * blocks + b]]
        rows_b = pl.ds(b * BLOCK, BLOCK)
        matrix = a_all[slot]
        low = jnp.dot(x_v[rows_b, :half], matrix, preferred_element_type=F32)
        high = jnp.dot(x_v[rows_b, half:], matrix, preferred_element_type=F32)
        return low, high

    for p in range(blocks // 2):
        low, high = shrink_pair(2 * p)
        low2, high2 = shrink_pair(2 * p + 1)
        both = jnp.where(
            lane < rank,
            low + pltpu.roll(high, rank, 1),
            pltpu.roll(low2, rank, 1) + high2,
        )
        packs[0, p] = both.astype(BF16)

    def pack_copy(k):
        return pltpu.make_async_remote_copy(
            src_ref=packs.at[0],
            dst_ref=packs.at[k],
            send_sem=pack_send.at[k],
            recv_sem=pack_recv.at[k],
            device_id={"tp": lax.rem(z + k, n)},
            device_id_type=MESH,
        )

    for k in range(1, n):
        pack_copy(k).start()

    lax.fori_loop(turn_b, n * per, step, 0)
    forward_table(*tables[1])

    for k in range(1, n):
        pack_copy(k).wait_recv()
    row = lax.broadcasted_iota(jnp.int32, (BLOCK, 128), 0)
    for p in range(blocks // 2):
        total = packs[0, p].astype(F32)
        for k in range(1, n):
            total = total + packs[k, p].astype(F32)
        for side in range(2):
            b = 2 * p + side
            mine = (lane < rank) if side == 0 else (lane >= rank)
            keep = mine & (row < live_ref[e * blocks + b])
            lhs[b] = jnp.where(keep, total, 0.0).astype(BF16)

    finish_table(*tables[1])
    for b in range(blocks):
        slot = table_ref[tenant_ref[e * blocks + b]]
        matrix = b_all[slot]
        stacked = jnp.concatenate([matrix, matrix], axis=0)
        for j in range(per):
            own[j, b * BLOCK : (b + 1) * BLOCK, :] += jnp.dot(
                lhs[b],
                stacked[:, j * chunk : (j + 1) * chunk],
                preferred_element_type=F32,
            )

    def out_place(j):
        return o_hbm.at[pl.ds(row0, rows), pl.ds(j * chunk, chunk)]

    def out_remote(j):
        return pltpu.make_async_remote_copy(
            src_ref=out_v.at[j],
            dst_ref=out_place(j),
            send_sem=out_send.at[j],
            recv_sem=out_recv.at[j],
            device_id=sibling,
            device_id_type=MESH,
        )

    for j in range(per):
        @pl.when(z < n - 1)
        def _():
            t = z * per + j
            left_copy(t).wait_recv()
            own[j] += left[t].astype(F32)

        @pl.when(z > 0)
        def _():
            t = (n - 1 - z) * per + j
            right_copy(t).wait_recv()
            own[j] += right[t].astype(F32)

        out_v[j] = own[j].astype(BF16)
        out_remote(j).start()
        pltpu.make_async_copy(out_v.at[j], out_place(j), out_local.at[j]).start()

    def right_done(t, carry):
        right_copy(t).wait_send()
        return carry

    def left_done(t, carry):
        left_copy(t).wait_send()
        return carry

    lax.fori_loop(0, n_right, right_done, 0)
    lax.fori_loop(0, n_left, left_done, 0)
    drain_table(*tables[0])
    drain_table(*tables[1])
    for k in range(1, n):
        pack_copy(k).wait_send()
    for j in range(per):
        out_remote(j).wait()
        pltpu.make_async_copy(out_v.at[j], out_place(j), out_local.at[j]).wait()


def per_device(
    n,
    n_sp,
    n_ep,
    activations,
    output_projection_weight,
    shrink_matrices,
    expand_matrices,
    tenant_of_block,
    token_rows_per_block,
    tenant_table_row,
):
    all_rows, depth = activations.shape
    rows = all_rows // n_ep
    width = expand_matrices.shape[2]
    chunk = min(CHUNK, width)
    per = width // chunk
    blocks = rows // BLOCK
    pieces, _, rank = shrink_matrices.shape
    count = pieces * n_sp * n_ep
    folded = jnp.concatenate(
        [shrink_matrices[:, : depth // 2], shrink_matrices[:, depth // 2 :]], axis=2
    )
    moving = (n - 1) * per
    dma = pltpu.SemaphoreType.DMA
    smem = pl.BlockSpec(memory_space=pltpu.SMEM)
    anywhere = pl.BlockSpec(memory_space=pl.ANY)
    return pl.pallas_call(
        functools.partial(kernel, n, n_sp, n_ep, chunk),
        out_shape=jax.ShapeDtypeStruct((all_rows, width), BF16),
        in_specs=[smem, smem, smem, anywhere, anywhere, anywhere, anywhere],
        out_specs=anywhere,
        scratch_shapes=[
            pltpu.VMEM((rows, depth), BF16),
            pltpu.VMEM((2, depth, chunk), BF16),
            pltpu.VMEM((rows, chunk), F32),
            pltpu.VMEM((moving, rows, chunk), BF16),
            pltpu.VMEM((moving, rows, chunk), BF16),
            pltpu.VMEM((per, rows, chunk), F32),
            pltpu.VMEM((per, rows, chunk), BF16),
            pltpu.VMEM((count, depth // 2, 2 * rank), BF16),
            pltpu.VMEM((count, rank, width), BF16),
            pltpu.VMEM((n, blocks // 2, BLOCK, 2 * rank), BF16),
            pltpu.VMEM((blocks, BLOCK, 2 * rank), BF16),
            dma,
            dma((2,)),
            dma((moving,)),
            dma((moving,)),
            dma((moving,)),
            dma((moving,)),
            dma,
            dma((2 * n_sp,)),
            dma((2 * n_sp,)),
            dma,
            dma((2 * n_sp,)),
            dma((2 * n_sp,)),
            dma((n,)),
            dma((n,)),
            dma((per,)),
            dma((per,)),
            dma((per,)),
        ],
        compiler_params=pltpu.CompilerParams(
            collective_id=0,
            has_side_effects=True,
            vmem_limit_bytes=56 * 1024 * 1024,
        ),
    )(
        tenant_of_block,
        token_rows_per_block,
        tenant_table_row,
        activations,
        output_projection_weight,
        folded,
        expand_matrices,
    )


def solution(mesh):
    in_specs = (
        P(("groups", "sp"), "tp"),
        P("tp", None),
        P(("sp", "ep"), "tp", None),
        P(("sp", "ep"), None, "tp"),
        P(("groups", "sp")),
        P(("groups", "sp")),
        P(),
    )
    return jax.shard_map(
        functools.partial(
            per_device, mesh.shape["tp"], mesh.shape["sp"], mesh.shape["ep"]
        ),
        mesh=mesh,
        in_specs=in_specs,
        out_specs=P(("groups", "sp"), "tp"),
        check_vma=False,
    )
```

time: 464 us -> 165 us (0.36)
  waiting for transfers between devices: 364 us -> 0 us
  Pallas kernels: 0 us -> 149 us
  matrix products: 76.3 us -> 0 us
  between operations: 13.1 us -> 0.02 us
  local copies, waits for them, and re-layouts: 0.64 us -> 11.3 us
    reduce_scatter x1 -> x0, waiting for transfers between devices: 278 us -> none  [per_device(): lax.psum_scatter(partial_term.astype(jnp.bfloat16), 'tp', scatter_dimensi...]
    pallas_call x0 -> x1, Pallas kernels: none -> 149 us  [per_device(): pl.pallas_call(functools.partial(kernel, n, n_sp, n_ep, chunk), out_shape...]
    dot_general x5 -> x0, matrix products: 76.3 us -> none  [the longest x1 41.8 us: per_device(): jnp.dot(activations, output_projection_weight, preferred_element_type=jnp...]
    all_gather x2 -> x0, waiting for transfers between devices: 62.7 us -> none  [the longest x1 60.5 us: per_device(): lax.all_gather(shrink_matrices, ('sp', 'ep'), axis=0, tiled=True)]
    psum x1 -> x0, waiting for transfers between devices: 21.7 us -> none  [per_device(): lax.psum(shrink_part.astype(jnp.bfloat16), 'tp').astype(jnp.float32)]
    convert_element_type x1 -> x0, other arithmetic: 8.29 us -> none  [per_device(): return (base + delta).astype(jnp.bfloat16)]
    unnamed x8 -> x3, local copies, waits for them, and re-layouts: 0.64 us -> 8.57 us
  transfers between devices with their start and end apart: 4 -> 0, of which waited for: 4 -> 0; matrix products, arithmetic and copies ran while one was open for 17% -> 0% of each run, Pallas kernels for 0% -> 0%
where the time goes in v1:
time: 165 us; the launch traced here: 164 us
  Pallas kernels  149 us (90%)
  local copies, waits for them, and re-layouts  11.3 us (7%)
  other arithmetic  4.06 us (2%)
    pallas_call x1, Pallas kernels, per_device(): pl.pallas_call(functools.partial(kernel, n, n_sp, n_ep, chunk), out_shape...  149 us
    unnamed x3, local copies, waits for them, and re-layouts  8.57 us
    concatenate x1, other arithmetic, per_device(): jnp.concatenate([shrink_matrices[:, :depth // 2], shrink_matrices[:, dept...  4.06 us

profile of v1, /device:TPU:17, one launch (start us, length us, event | category | flops | bytes accessed | tf_op | source)
XLA Modules:
  0.0 164.2 jit_solution(4317504189009931427)
XLA Ops:
  0.0 2.8 %fusion = (bf16[8,1024,64]{1,2,0:T(8,128)(2,1)}, bf16[8,1024,64]{1,2,0:T(8,128)(2,1)S(1)}) fusion(bf16[8,2048,64]{1,2,0:T(8,128)(2,1)} %param.9), kind=kLoop, calls=%fused_computation.1 | loop fusion | bytes 4194304 | tf_op jit(solution)/shard_map/slice | solution.py:384
  2.8 2.0 %copy.10 = bf16[8,1024,64]{2,1,0:T(8,128)(2,1)S(1)} copy(bf16[8,1024,64]{1,2,0:T(8,128)(2,1)} %get-tuple-element.5) | data formatting | bytes 2097152
  4.8 1.8 %copy.11 = bf16[8,1024,64]{2,1,0:T(8,128)(2,1)} copy(bf16[8,1024,64]{1,2,0:T(8,128)(2,1)S(1)} %get-tuple-element.6) | data formatting | bytes 2097152
  6.6 4.1 %pad_maximum_fusion.a_hbm = bf16[8,1024,128]{2,1,0:T(8,128)(2,1)} fusion(bf16[8,1024,64]{2,1,0:T(8,128)(2,1)} %copy.11, bf16[8,1024,64]{2,1,0:T(8,128)(2,1)S(1)} %copy.10), kind=kLoop, calls=%fused_computation | loop fusion | flops 4194304 | bytes 4194304 | tf_op jit(solution)/shard_map/concatenate | solution.py:383
  10.6 148.8 %shard_map.73 = bf16[1024,2048]{1,0:T(8,128)(2,1)} custom-call(s32[8]{0:T(128)} %tenant_ref.1, s32[8]{0:T(128)} %live_ref.1, s32[32]{0:T(128)} %table_ref.1, bf16[1024,2048]{1,0:T(8,128)(2,1)} %x_hbm.1, bf16[2048,8192]{1,0:T(8,128)(2,1)} %w_hbm.1, bf16[8,1024,128]{2,1,0:T(8,128)(2,1)} %pad_maximum_fusion.a_hbm, bf16[8,64,2048]{2,1,0:T(8,128)(2,1)} %b_hbm.1), custom_call_target="tpu_custom_call" | custom-call | tf_op jit(solution)/shard_map/pallas_call | solution.py:390
  159.4 4.8 %copy.13 = bf16[1024,2048]{1,0:T(8,128)(2,1)} copy(bf16[1024,2048]{1,0:T(8,128)(2,1)} %shard_map.73) | data formatting | bytes 8388608

commit v2 on v1

--- a/solution.py
+++ b/solution.py
@@ -8,7 +8,7 @@
 from jax.sharding import PartitionSpec as P
 
 BLOCK = 128
-CHUNK = 512
+CHUNK = 256
 MESH = pl.DeviceIdType.MESH
 F32 = jnp.float32
 BF16 = jnp.bfloat16
@@ -26,17 +26,20 @@
     w_hbm,
     a_hbm,
     b_hbm,
-    o_hbm,
+    o_ref,
     x_v,
     w_v,
     prod,
     right,
     left,
     own,
-    out_v,
     a_all,
     b_all,
     packs,
+    from_left,
+    from_right,
+    pack_right,
+    pack_left,
     lhs,
     x_sem,
     w_sem,
@@ -52,16 +55,14 @@
     b_recv,
     pack_send,
     pack_recv,
-    out_local,
     out_send,
     out_recv,
 ):
     z = lax.axis_index("tp")
     s = lax.axis_index("sp")
     e = lax.axis_index("ep")
-    rows, depth = x_v.shape
-    half = depth // 2
-    width = o_hbm.shape[1]
+    rows = x_v.shape[0]
+    width = o_ref.shape[1]
     per = width // chunk
     blocks = rows // BLOCK
     pieces = a_hbm.shape[0]
@@ -195,6 +196,26 @@
             device_id_type=MESH,
         )
 
+    def pack_right_copy():
+        return pltpu.make_async_remote_copy(
+            src_ref=pack_right,
+            dst_ref=pack_right,
+            send_sem=pack_send.at[0],
+            recv_sem=pack_recv.at[0],
+            device_id={"tp": z + 1},
+            device_id_type=MESH,
+        )
+
+    def pack_left_copy():
+        return pltpu.make_async_remote_copy(
+            src_ref=pack_left,
+            dst_ref=pack_left,
+            send_sem=pack_send.at[1],
+            recv_sem=pack_recv.at[1],
+            device_id={"tp": z - 1},
+            device_id_type=MESH,
+        )
+
     def step(i, carry):
         kind, t = item(i)
         slot = i % 2
@@ -238,61 +259,88 @@
 
         return carry
 
-    start_table(*tables[0])
     x_copy.wait()
     step(0, 0)
+    start_table(*tables[0])
     start_table(*tables[1])
-    turn_a = min(5, moving)
-    turn_b = min(7, moving)
+    turn_a = max(1, moving * 5 // 12)
+    turn_b = max(1, moving * 7 // 12)
     lax.fori_loop(1, turn_a, step, 0)
     forward_table(*tables[0])
     lax.fori_loop(turn_a, turn_b, step, 0)
     finish_table(*tables[0])
 
-    lane = lax.broadcasted_iota(jnp.int32, (BLOCK, 128), 1)
-    rank = lane.shape[1] // 2
-
-    def shrink_pair(b):
+    rank = b_hbm.shape[1]
+    lane = lax.broadcasted_iota(jnp.int32, (BLOCK, 2 * rank), 1)
+
+    def shrink_twice(b):
         slot = table_ref[tenant_ref[e * blocks + b]]
-        rows_b = pl.ds(b * BLOCK, BLOCK)
         matrix = a_all[slot]
-        low = jnp.dot(x_v[rows_b, :half], matrix, preferred_element_type=F32)
-        high = jnp.dot(x_v[rows_b, half:], matrix, preferred_element_type=F32)
-        return low, high
+        return lax.dot_general(
+            x_v[b * BLOCK : (b + 1) * BLOCK, :],
+            jnp.concatenate([matrix, matrix], axis=0),
+            (((1,), (1,)), ((), ())),
+            preferred_element_type=F32,
+        )
 
     for p in range(blocks // 2):
-        low, high = shrink_pair(2 * p)
-        low2, high2 = shrink_pair(2 * p + 1)
-        both = jnp.where(
-            lane < rank,
-            low + pltpu.roll(high, rank, 1),
-            pltpu.roll(low2, rank, 1) + high2,
-        )
-        packs[0, p] = both.astype(BF16)
-
-    def pack_copy(k):
-        return pltpu.make_async_remote_copy(
-            src_ref=packs.at[0],
-            dst_ref=packs.at[k],
-            send_sem=pack_send.at[k],
-            recv_sem=pack_recv.at[k],
-            device_id={"tp": lax.rem(z + k, n)},
-            device_id_type=MESH,
-        )
-
-    for k in range(1, n):
-        pack_copy(k).start()
-
-    lax.fori_loop(turn_b, n * per, step, 0)
+        packs[p] = jnp.where(
+            lane < rank, shrink_twice(2 * p), shrink_twice(2 * p + 1)
+        )
+
+    @pl.when(z == 0)
+    def _():
+        pack_right[...] = packs[...].astype(BF16)
+        pack_right_copy().start()
+
+    @pl.when(z == n - 1)
+    def _():
+        pack_left[...] = packs[...].astype(BF16)
+        pack_left_copy().start()
+
+    lax.fori_loop(turn_b, moving, step, 0)
+
+    def pass_right():
+        @pl.when(z > 0)
+        def _():
+            pack_right_copy().wait_recv()
+            from_left[...] = pack_right[...].astype(F32)
+
+            @pl.when(z < n - 1)
+            def _():
+                pack_right[...] = (packs[...] + from_left[...]).astype(BF16)
+                pack_right_copy().start()
+
+    def pass_left():
+        @pl.when(z < n - 1)
+        def _():
+            pack_left_copy().wait_recv()
+            from_right[...] = pack_left[...].astype(F32)
+
+            @pl.when(z > 0)
+            def _():
+                pack_left[...] = (packs[...] + from_right[...]).astype(BF16)
+                pack_left_copy().start()
+
+    from_left[...] = jnp.zeros_like(from_left)
+    from_right[...] = jnp.zeros_like(from_right)
+
+    @pl.when(in_low)
+    def _():
+        pass_right()
+
+    pass_left()
+
+    @pl.when(jnp.logical_not(in_low))
+    def _():
+        pass_right()
+
+    lax.fori_loop(moving, n * per, step, 0)
     forward_table(*tables[1])
 
-    for k in range(1, n):
-        pack_copy(k).wait_recv()
-    row = lax.broadcasted_iota(jnp.int32, (BLOCK, 128), 0)
+    row = lax.broadcasted_iota(jnp.int32, (BLOCK, 2 * rank), 0)
     for p in range(blocks // 2):
-        total = packs[0, p].astype(F32)
-        for k in range(1, n):
-            total = total + packs[k, p].astype(F32)
+        total = packs[p] + from_left[p] + from_right[p]
         for side in range(2):
             b = 2 * p + side
             mine = (lane < rank) if side == 0 else (lane >= rank)
@@ -311,13 +359,11 @@
                 preferred_element_type=F32,
             )
 
-    def out_place(j):
-        return o_hbm.at[pl.ds(row0, rows), pl.ds(j * chunk, chunk)]
-
     def out_remote(j):
-        return pltpu.make_async_remote_copy(
-            src_ref=out_v.at[j],
-            dst_ref=out_place(j),
+        place = o_ref.at[pl.ds(row0, rows), pl.ds(j * chunk, chunk)]
+        return pltpu.make_async_remote_copy(
+            src_ref=place,
+            dst_ref=place,
             send_sem=out_send.at[j],
             recv_sem=out_recv.at[j],
             device_id=sibling,
@@ -337,9 +383,8 @@
             right_copy(t).wait_recv()
             own[j] += right[t].astype(F32)
 
-        out_v[j] = own[j].astype(BF16)
+        o_ref[pl.ds(row0, rows), j * chunk : (j + 1) * chunk] = own[j].astype(BF16)
         out_remote(j).start()
-        pltpu.make_async_copy(out_v.at[j], out_place(j), out_local.at[j]).start()
 
     def right_done(t, carry):
         right_copy(t).wait_send()
@@ -353,11 +398,17 @@
     lax.fori_loop(0, n_left, left_done, 0)
     drain_table(*tables[0])
     drain_table(*tables[1])
-    for k in range(1, n):
-        pack_copy(k).wait_send()
+
+    @pl.when(z < n - 1)
+    def _():
+        pack_right_copy().wait_send()
+
+    @pl.when(z > 0)
+    def _():
+        pack_left_copy().wait_send()
+
     for j in range(per):
         out_remote(j).wait()
-        pltpu.make_async_copy(out_v.at[j], out_place(j), out_local.at[j]).wait()
 
 
 def per_device(
@@ -380,18 +431,17 @@
     blocks = rows // BLOCK
     pieces, _, rank = shrink_matrices.shape
     count = pieces * n_sp * n_ep
-    folded = jnp.concatenate(
-        [shrink_matrices[:, : depth // 2], shrink_matrices[:, depth // 2 :]], axis=2
-    )
+    turned = jnp.swapaxes(shrink_matrices, 1, 2)
+    pack = (blocks // 2, BLOCK, 2 * rank)
     moving = (n - 1) * per
     dma = pltpu.SemaphoreType.DMA
     smem = pl.BlockSpec(memory_space=pltpu.SMEM)
     anywhere = pl.BlockSpec(memory_space=pl.ANY)
     return pl.pallas_call(
         functools.partial(kernel, n, n_sp, n_ep, chunk),
-        out_shape=jax.ShapeDtypeStruct((all_rows, width), BF16),
+        out_shape=pltpu.VMEM((all_rows, width), BF16),
         in_specs=[smem, smem, smem, anywhere, anywhere, anywhere, anywhere],
-        out_specs=anywhere,
+        out_specs=pl.BlockSpec(memory_space=pltpu.VMEM),
         scratch_shapes=[
             pltpu.VMEM((rows, depth), BF16),
             pltpu.VMEM((2, depth, chunk), BF16),
@@ -399,10 +449,13 @@
             pltpu.VMEM((moving, rows, chunk), BF16),
             pltpu.VMEM((moving, rows, chunk), BF16),
             pltpu.VMEM((per, rows, chunk), F32),
-            pltpu.VMEM((per, rows, chunk), BF16),
-            pltpu.VMEM((count, depth // 2, 2 * rank), BF16),
+            pltpu.VMEM((count, rank, depth), BF16),
             pltpu.VMEM((count, rank, width), BF16),
-            pltpu.VMEM((n, blocks // 2, BLOCK, 2 * rank), BF16),
+            pltpu.VMEM(pack, F32),
+            pltpu.VMEM(pack, F32),
+            pltpu.VMEM(pack, F32),
+            pltpu.VMEM(pack, BF16),
+            pltpu.VMEM(pack, BF16),
             pltpu.VMEM((blocks, BLOCK, 2 * rank), BF16),
             dma,
             dma((2,)),
@@ -416,16 +469,15 @@
             dma,
             dma((2 * n_sp,)),
             dma((2 * n_sp,)),
-            dma((n,)),
-            dma((n,)),
-            dma((per,)),
+            dma((2,)),
+            dma((2,)),
             dma((per,)),
             dma((per,)),
         ],
         compiler_params=pltpu.CompilerParams(
             collective_id=0,
             has_side_effects=True,
-            vmem_limit_bytes=56 * 1024 * 1024,
+            vmem_limit_bytes=48 * 1024 * 1024,
         ),
     )(
         tenant_of_block,
@@ -433,7 +485,7 @@
         tenant_table_row,
         activations,
         output_projection_weight,
-        folded,
+        turned,
         expand_matrices,
     )
 

time: 165 us -> 150 us (0.909)
  local copies, waits for them, and re-layouts: 11.3 us -> 3.98 us
  other arithmetic: 4.06 us -> 0 us
  Pallas kernels: 149 us -> 145 us
    unnamed x3 -> x7, local copies, waits for them, and re-layouts: 8.57 us -> 3.98 us
    pallas_call x1, Pallas kernels: 149 us -> 145 us  [per_device(): pl.pallas_call(functools.partial(kernel, n, n_sp, n_ep, chunk), out_shape...]
    concatenate x1 -> x0, other arithmetic: 4.06 us -> none  [per_device(): jnp.concatenate([shrink_matrices[:, :depth // 2], shrink_matrices[:, dept...]
    slice x1 -> x0, local copies, waits for them, and re-layouts: 2.76 us -> none  [per_device(): shrink_matrices[:, :depth // 2]]
where the time goes in v2:
time: 150 us; the launch traced here: 149 us
  Pallas kernels  145 us (97%)
  local copies, waits for them, and re-layouts  3.98 us (3%)
    pallas_call x1, Pallas kernels, per_device(): pl.pallas_call(functools.partial(kernel, n, n_sp, n_ep, chunk), out_shape...  145 us
    unnamed x7, local copies, waits for them, and re-layouts  3.98 us

profile of v2, /device:TPU:17, one launch (start us, length us, event | category | flops | bytes accessed | tf_op | source)
XLA Modules:
  0.0 148.7 jit_solution(2726847655255503781)
XLA Ops:
  0.0 0.0 copy-start
  0.0 0.7 copy-done
  0.7 0.0 copy-start.1
  0.7 0.7 copy-done.1
  1.3 0.0 copy-start.2
  1.3 0.7 copy-done.2
  2.0 144.7 %shard_map.73 = bf16[1024,2048]{1,0:T(8,128)(2,1)S(1)} custom-call(s32[8]{0:T(128)S(1)} %copy-done, s32[8]{0:T(128)S(1)} %copy-done.1, s32[32]{0:T(128)S(1)} %copy-done.2, bf16[1024,2048]{1,0:T(8,128)(2,1)} %x_hbm.1, bf16[2048,8192]{1,0:T(8,128)(2,1)} %w_hbm.1, bf16[8,64,2048]{2,1,0:T(8,128)(2,1)} %bitcast.1, bf16[8,64,2048]{2,1,0:T(8,128)(2,1)} %b_hbm.1), custom_call_target="tpu_custom_call" | custom-call | tf_op jit(solution)/shard_map/pallas_call | solution.py:440
  146.7 2.0 %copy.9 = bf16[1024,2048]{1,0:T(8,128)(2,1)} copy(bf16[1024,2048]{1,0:T(8,128)(2,1)S(1)} %shard_map.73) | data formatting | bytes 8388608
Async XLA Ops:
  0.0 0.7 copy-start
  0.7 0.7 copy-start.1
  1.3 0.7 copy-start.2

commit v3 on v2

--- a/solution.py
+++ b/solution.py
@@ -19,14 +19,17 @@
     n_sp,
     n_ep,
     chunk,
-    tenant_ref,
-    live_ref,
-    table_ref,
+    tenant_hbm,
+    live_hbm,
+    table_hbm,
     x_hbm,
     w_hbm,
     a_hbm,
     b_hbm,
     o_ref,
+    tenant_ref,
+    live_ref,
+    table_ref,
     x_v,
     w_v,
     prod,
@@ -41,6 +44,7 @@
     pack_right,
     pack_left,
     lhs,
+    int_sem,
     x_sem,
     w_sem,
     right_send,
@@ -107,20 +111,32 @@
 
     w_copy(0).start()
 
+    int_copies = [
+        pltpu.make_async_copy(src, dst, int_sem.at[k])
+        for k, (src, dst) in enumerate(
+            ((tenant_hbm, tenant_ref), (live_hbm, live_ref), (table_hbm, table_ref))
+        )
+    ]
+
     barrier = pltpu.get_barrier_semaphore()
-    for k in range(1, n):
-        pl.semaphore_signal(
-            barrier, inc=1, device_id={"tp": lax.rem(z + k, n)}, device_id_type=MESH
-        )
+
+    def greet(device_id):
+        pl.semaphore_signal(barrier, inc=1, device_id=device_id, device_id_type=MESH)
+
+    @pl.when(z > 0)
+    def _():
+        greet({"tp": z - 1})
+
+    @pl.when(z < n - 1)
+    def _():
+        greet({"tp": z + 1})
+
     for k in range(1, n_sp):
-        pl.semaphore_signal(
-            barrier, inc=1, device_id={"sp": lax.rem(s + k, n_sp)}, device_id_type=MESH
-        )
+        greet({"sp": lax.rem(s + k, n_sp)})
     for k in range(1, n_ep):
-        pl.semaphore_signal(
-            barrier, inc=1, device_id={"ep": lax.rem(e + k, n_ep)}, device_id_type=MESH
-        )
-    pl.semaphore_wait(barrier, n + n_sp + n_ep - 3)
+        greet({"ep": lax.rem(e + k, n_ep)})
+    along_line = jnp.where(z > 0, 1, 0) + jnp.where(z < n - 1, 1, 0)
+    greeters = along_line + (n_sp - 1) + (n_ep - 1)
 
     sibling = {"ep": lax.rem(e + 1, n_ep)}
 
@@ -216,8 +232,7 @@
             device_id_type=MESH,
         )
 
-    def step(i, carry):
-        kind, t = item(i)
+    def multiply(i):
         slot = i % 2
 
         @pl.when(i + 1 < n * per)
@@ -226,6 +241,9 @@
 
         w_copy(i).wait()
         prod[...] = jnp.dot(x_v[...], w_v[slot], preferred_element_type=F32)
+
+    def pass_on(i):
+        kind, t = item(i)
 
         @pl.when(kind == 0)
         def _():
@@ -257,18 +275,27 @@
         def _():
             own[t] = prod[...]
 
+    def step(i, carry):
+        multiply(i)
+        pass_on(i)
         return carry
 
     x_copy.wait()
-    step(0, 0)
+    multiply(0)
+    pl.semaphore_wait(barrier, greeters)
+    pass_on(0)
     start_table(*tables[0])
     start_table(*tables[1])
+    for copy in int_copies:
+        copy.start()
     turn_a = max(1, moving * 5 // 12)
     turn_b = max(1, moving * 7 // 12)
     lax.fori_loop(1, turn_a, step, 0)
     forward_table(*tables[0])
     lax.fori_loop(turn_a, turn_b, step, 0)
     finish_table(*tables[0])
+    for copy in int_copies:
+        copy.wait()
 
     rank = b_hbm.shape[1]
     lane = lax.broadcasted_iota(jnp.int32, (BLOCK, 2 * rank), 1)
@@ -370,21 +397,43 @@
             device_id_type=MESH,
         )
 
-    for j in range(per):
+    def take_left(j):
+        left_copy(z * per + j).wait_recv()
+        return left[z * per + j].astype(F32)
+
+    def take_right(j):
+        t = (n - 1 - z) * per + j
+        right_copy(t).wait_recv()
+        return right[t].astype(F32)
+
+    def finish(j, value):
+        o_ref[pl.ds(row0, rows), j * chunk : (j + 1) * chunk] = value.astype(BF16)
+        out_remote(j).start()
+
+    @pl.when(in_low)
+    def _():
+        for j in range(per):
+            own[j] += take_left(j)
+
+        @pl.when(z > 0)
+        def _():
+            for j in range(per):
+                finish(j, own[j] + take_right(j))
+
+    @pl.when(jnp.logical_not(in_low))
+    def _():
+        for j in range(per):
+            own[j] += take_right(j)
+
         @pl.when(z < n - 1)
         def _():
-            t = z * per + j
-            left_copy(t).wait_recv()
-            own[j] += left[t].astype(F32)
-
-        @pl.when(z > 0)
-        def _():
-            t = (n - 1 - z) * per + j
-            right_copy(t).wait_recv()
-            own[j] += right[t].astype(F32)
-
-        o_ref[pl.ds(row0, rows), j * chunk : (j + 1) * chunk] = own[j].astype(BF16)
-        out_remote(j).start()
+            for j in range(per):
+                finish(j, own[j] + take_left(j))
+
+    @pl.when((z == 0) | (z == n - 1))
+    def _():
+        for j in range(per):
+            finish(j, own[j])
 
     def right_done(t, carry):
         right_copy(t).wait_send()
@@ -435,14 +484,16 @@
     pack = (blocks // 2, BLOCK, 2 * rank)
     moving = (n - 1) * per
     dma = pltpu.SemaphoreType.DMA
-    smem = pl.BlockSpec(memory_space=pltpu.SMEM)
-    anywhere = pl.BlockSpec(memory_space=pl.ANY)
+    in_hbm = pl.BlockSpec(memory_space=pltpu.HBM)
     return pl.pallas_call(
         functools.partial(kernel, n, n_sp, n_ep, chunk),
         out_shape=pltpu.VMEM((all_rows, width), BF16),
-        in_specs=[smem, smem, smem, anywhere, anywhere, anywhere, anywhere],
+        in_specs=[in_hbm] * 7,
         out_specs=pl.BlockSpec(memory_space=pltpu.VMEM),
         scratch_shapes=[
+            pltpu.SMEM(tenant_of_block.shape, jnp.int32),
+            pltpu.SMEM(token_rows_per_block.shape, jnp.int32),
+            pltpu.SMEM(tenant_table_row.shape, jnp.int32),
             pltpu.VMEM((rows, depth), BF16),
             pltpu.VMEM((2, depth, chunk), BF16),
             pltpu.VMEM((rows, chunk), F32),
@@ -457,6 +508,7 @@
             pltpu.VMEM(pack, BF16),
             pltpu.VMEM(pack, BF16),
             pltpu.VMEM((blocks, BLOCK, 2 * rank), BF16),
+            dma((3,)),
             dma,
             dma((2,)),
             dma((moving,)),

time: 150 us -> 149 us (level)
  no operation moved by 1% of the time
where the time goes in v3:
time: 149 us; the launch traced here: 148 us
  Pallas kernels  144 us (97%)
  local copies, waits for them, and re-layouts  3.98 us (3%)
    pallas_call x1, Pallas kernels, per_device(): pl.pallas_call(functools.partial(kernel, n, n_sp, n_ep, chunk), out_shape...  144 us
    unnamed x7, local copies, waits for them, and re-layouts  3.98 us

profile of v3, /device:TPU:17, one launch (start us, length us, event | category | flops | bytes accessed | tf_op | source)
XLA Modules:
  0.0 148.1 jit_solution(15788827898453849736)
XLA Ops:
  0.0 0.0 copy-start
  0.0 0.7 copy-done
  0.7 0.0 copy-start.1
  0.7 0.7 copy-done.1
  1.3 0.0 copy-start.2
  1.3 0.7 copy-done.2
  2.0 144.1 %shard_map.73 = bf16[1024,2048]{1,0:T(8,128)(2,1)S(1)} custom-call(s32[8]{0:T(128)S(1)} %copy-done, s32[8]{0:T(128)S(1)} %copy-done.1, s32[32]{0:T(128)S(1)} %copy-done.2, bf16[1024,2048]{1,0:T(8,128)(2,1)} %x_hbm.1, bf16[2048,8192]{1,0:T(8,128)(2,1)} %w_hbm.1, bf16[8,64,2048]{2,1,0:T(8,128)(2,1)} %bitcast.1, bf16[8,64,2048]{2,1,0:T(8,128)(2,1)} %b_hbm.1), custom_call_target="tpu_custom_call" | custom-call | tf_op jit(solution)/shard_map/pallas_call | solution.py:488
  146.1 2.0 %copy.9 = bf16[1024,2048]{1,0:T(8,128)(2,1)} copy(bf16[1024,2048]{1,0:T(8,128)(2,1)S(1)} %shard_map.73) | data formatting | bytes 8388608
Async XLA Ops:
  0.0 0.7 copy-start
  0.7 0.7 copy-start.1
  1.3 0.7 copy-start.2

commit v4 on v3

--- a/solution.py
+++ b/solution.py
@@ -8,7 +8,8 @@
 from jax.sharding import PartitionSpec as P
 
 BLOCK = 128
-CHUNK = 256
+CHUNK = 512
+ENDS = 4
 MESH = pl.DeviceIdType.MESH
 F32 = jnp.float32
 BF16 = jnp.bfloat16
@@ -51,6 +52,10 @@
     right_recv,
     left_send,
     left_recv,
+    end_right_send,
+    end_right_recv,
+    end_left_send,
+    end_left_recv,
     a_local,
     a_send,
     a_recv,
@@ -73,8 +78,14 @@
     moving = (n - 1) * per
     row0 = pl.multiple_of(e * rows, BLOCK)
 
-    x_copy = pltpu.make_async_copy(x_hbm.at[pl.ds(row0, rows), :], x_v, x_sem)
-    x_copy.start()
+    half = rows // 2
+    halves = [pl.ds(h * half, half) for h in range(2)]
+    x_copies = [
+        pltpu.make_async_copy(
+            x_hbm.at[pl.ds(row0 + h * half, half), :], x_v.at[halves[h]], x_sem.at[h]
+        )
+        for h in range(2)
+    ]
 
     n_right = (n - 1 - z) * per
     n_left = z * per
@@ -110,6 +121,8 @@
         )
 
     w_copy(0).start()
+    for copy in x_copies:
+        copy.start()
 
     int_copies = [
         pltpu.make_async_copy(src, dst, int_sem.at[k])
@@ -135,8 +148,8 @@
         greet({"sp": lax.rem(s + k, n_sp)})
     for k in range(1, n_ep):
         greet({"ep": lax.rem(e + k, n_ep)})
-    along_line = jnp.where(z > 0, 1, 0) + jnp.where(z < n - 1, 1, 0)
-    greeters = along_line + (n_sp - 1) + (n_ep - 1)
+    line_ends = jnp.where(z > 0, 1, 0) + jnp.where(z < n - 1, 1, 0)
+    greeters = line_ends + (n_sp - 1) + (n_ep - 1)
 
     sibling = {"ep": lax.rem(e + 1, n_ep)}
 
@@ -192,24 +205,34 @@
         for k in range(n_sp):
             along_ep(src, gathered, send, recv, k).wait_send()
 
-    def right_copy(t):
+    def along_line(ref, t, send, recv, to, place=None):
+        piece = ref.at[t] if place is None else ref.at[t, place]
         return pltpu.make_async_remote_copy(
-            src_ref=right.at[t],
-            dst_ref=right.at[t],
-            send_sem=right_send.at[t],
-            recv_sem=right_recv.at[t],
-            device_id={"tp": z + 1},
+            src_ref=piece,
+            dst_ref=piece,
+            send_sem=send,
+            recv_sem=recv,
+            device_id={"tp": to},
             device_id_type=MESH,
         )
 
-    def left_copy(t):
-        return pltpu.make_async_remote_copy(
-            src_ref=left.at[t],
-            dst_ref=left.at[t],
-            send_sem=left_send.at[t],
-            recv_sem=left_recv.at[t],
-            device_id={"tp": z - 1},
-            device_id_type=MESH,
+    def right_copy(t, place=None):
+        return along_line(right, t, right_send.at[t], right_recv.at[t], z + 1, place)
+
+    def left_copy(t, place=None):
+        return along_line(left, t, left_send.at[t], left_recv.at[t], z - 1, place)
+
+    fine = rows // ENDS
+    parts = [pl.ds(q * fine, fine) for q in range(ENDS)]
+
+    def right_end(t, q):
+        return along_line(
+            right, t, end_right_send.at[q], end_right_recv.at[q], z + 1, parts[q]
+        )
+
+    def left_end(t, q):
+        return along_line(
+            left, t, end_left_send.at[q], end_left_recv.at[q], z - 1, parts[q]
         )
 
     def pack_right_copy():
@@ -256,7 +279,14 @@
             def _():
                 right[t] = prod[...].astype(BF16)
 
-            right_copy(t).start()
+            @pl.when(t < n_right - 1)
+            def _():
+                right_copy(t).start()
+
+            @pl.when(t == n_right - 1)
+            def _():
+                for q in range(ENDS):
+                    right_end(t, q).start()
 
         @pl.when(kind == 1)
         def _():
@@ -269,7 +299,14 @@
             def _():
                 left[t] = prod[...].astype(BF16)
 
-            left_copy(t).start()
+            @pl.when(t < n_left - 1)
+            def _():
+                left_copy(t).start()
+
+            @pl.when(t == n_left - 1)
+            def _():
+                for q in range(ENDS):
+                    left_end(t, q).start()
 
         @pl.when(kind == 2)
         def _():
@@ -280,10 +317,30 @@
         pass_on(i)
         return carry
 
-    x_copy.wait()
-    multiply(0)
-    pl.semaphore_wait(barrier, greeters)
-    pass_on(0)
+    w_copy(1).start()
+    w_copy(0).wait()
+    for h in range(2):
+        x_copies[h].wait()
+        prod[halves[h], :] = jnp.dot(
+            x_v[halves[h], :], w_v[0], preferred_element_type=F32
+        )
+        if h == 0:
+            pl.semaphore_wait(barrier, greeters)
+
+        @pl.when(z == 0)
+        def _():
+            right[0, halves[h], :] = prod[halves[h], :].astype(BF16)
+            right_copy(0, halves[h]).start()
+
+        @pl.when(z == n - 1)
+        def _():
+            left[0, halves[h], :] = prod[halves[h], :].astype(BF16)
+            left_copy(0, halves[h]).start()
+
+    @pl.when((z > 0) & (z < n - 1))
+    def _():
+        pass_on(0)
+
     start_table(*tables[0])
     start_table(*tables[1])
     for copy in int_copies:
@@ -386,54 +443,68 @@
                 preferred_element_type=F32,
             )
 
-    def out_remote(j):
-        place = o_ref.at[pl.ds(row0, rows), pl.ds(j * chunk, chunk)]
+    whole = [pl.ds(0, rows)]
+
+    def spans(j):
+        return parts if j == per - 1 else whole
+
+    def out_remote(j, q):
+        span = spans(j)[q]
+        place = o_ref.at[
+            pl.ds(pl.multiple_of(row0 + span.start, span.size), span.size),
+            pl.ds(j * chunk, chunk),
+        ]
         return pltpu.make_async_remote_copy(
             src_ref=place,
             dst_ref=place,
-            send_sem=out_send.at[j],
-            recv_sem=out_recv.at[j],
+            send_sem=out_send.at[j + q],
+            recv_sem=out_recv.at[j + q],
             device_id=sibling,
             device_id_type=MESH,
         )
 
-    def take_left(j):
-        left_copy(z * per + j).wait_recv()
-        return left[z * per + j].astype(F32)
-
-    def take_right(j):
+    def take_left(j, q):
+        t = z * per + j
+        (left_end(t, q) if j == per - 1 else left_copy(t)).wait_recv()
+        return left[t, spans(j)[q], :].astype(F32)
+
+    def take_right(j, q):
         t = (n - 1 - z) * per + j
-        right_copy(t).wait_recv()
-        return right[t].astype(F32)
-
-    def finish(j, value):
-        o_ref[pl.ds(row0, rows), j * chunk : (j + 1) * chunk] = value.astype(BF16)
-        out_remote(j).start()
+        (right_end(t, q) if j == per - 1 else right_copy(t)).wait_recv()
+        return right[t, spans(j)[q], :].astype(F32)
+
+    def finish(j, q, value):
+        span = spans(j)[q]
+        start = pl.multiple_of(row0 + span.start, span.size)
+        o_ref[pl.ds(start, span.size), j * chunk : (j + 1) * chunk] = value.astype(BF16)
+        out_remote(j, q).start()
+
+    pieces_out = [(j, q) for j in range(per) for q in range(len(spans(j)))]
 
     @pl.when(in_low)
     def _():
-        for j in range(per):
-            own[j] += take_left(j)
+        for j, q in pieces_out:
+            own[j, spans(j)[q], :] += take_left(j, q)
 
         @pl.when(z > 0)
         def _():
-            for j in range(per):
-                finish(j, own[j] + take_right(j))
+            for j, q in pieces_out:
+                finish(j, q, own[j, spans(j)[q], :] + take_right(j, q))
 
     @pl.when(jnp.logical_not(in_low))
     def _():
-        for j in range(per):
-            own[j] += take_right(j)
+        for j, q in pieces_out:
+            own[j, spans(j)[q], :] += take_right(j, q)
 
         @pl.when(z < n - 1)
         def _():
-            for j in range(per):
-                finish(j, own[j] + take_left(j))
+            for j, q in pieces_out:
+                finish(j, q, own[j, spans(j)[q], :] + take_left(j, q))
 
     @pl.when((z == 0) | (z == n - 1))
     def _():
-        for j in range(per):
-            finish(j, own[j])
+        for j, q in pieces_out:
+            finish(j, q, own[j, spans(j)[q], :])
 
     def right_done(t, carry):
         right_copy(t).wait_send()
@@ -443,21 +514,25 @@
         left_copy(t).wait_send()
         return carry
 
-    lax.fori_loop(0, n_right, right_done, 0)
-    lax.fori_loop(0, n_left, left_done, 0)
+    lax.fori_loop(0, n_right - 1, right_done, 0)
+    lax.fori_loop(0, n_left - 1, left_done, 0)
     drain_table(*tables[0])
     drain_table(*tables[1])
 
     @pl.when(z < n - 1)
     def _():
+        for q in range(ENDS):
+            right_end(n_right - 1, q).wait_send()
         pack_right_copy().wait_send()
 
     @pl.when(z > 0)
     def _():
+        for q in range(ENDS):
+            left_end(n_left - 1, q).wait_send()
         pack_left_copy().wait_send()
 
-    for j in range(per):
-        out_remote(j).wait()
+    for j, q in pieces_out:
+        out_remote(j, q).wait()
 
 
 def per_device(
@@ -509,12 +584,16 @@
             pltpu.VMEM(pack, BF16),
             pltpu.VMEM((blocks, BLOCK, 2 * rank), BF16),
             dma((3,)),
-            dma,
+            dma((2,)),
             dma((2,)),
             dma((moving,)),
             dma((moving,)),
             dma((moving,)),
             dma((moving,)),
+            dma((ENDS,)),
+            dma((ENDS,)),
+            dma((ENDS,)),
+            dma((ENDS,)),
             dma,
             dma((2 * n_sp,)),
             dma((2 * n_sp,)),
@@ -523,8 +602,8 @@
             dma((2 * n_sp,)),
             dma((2,)),
             dma((2,)),
-            dma((per,)),
-            dma((per,)),
+            dma((per - 1 + ENDS,)),
+            dma((per - 1 + ENDS,)),
         ],
         compiler_params=pltpu.CompilerParams(
             collective_id=0,
@@ -532,9 +611,9 @@
             vmem_limit_bytes=48 * 1024 * 1024,
         ),
     )(
-        tenant_of_block,
-        token_rows_per_block,
-        tenant_table_row,
+        pltpu.with_memory_space_constraint(tenant_of_block, pltpu.HBM),
+        pltpu.with_memory_space_constraint(token_rows_per_block, pltpu.HBM),
+        pltpu.with_memory_space_constraint(tenant_table_row, pltpu.HBM),
         activations,
         output_projection_weight,
         turned,

time: 149 us -> 146 us (0.980)
  local copies, waits for them, and re-layouts: 3.98 us -> 2.02 us
    unnamed x7 -> x1, local copies, waits for them, and re-layouts: 3.98 us -> 2.02 us
where the time goes in v4:
time: 146 us
  Pallas kernels  144 us (99%)
  local copies, waits for them, and re-layouts  2.02 us (1%)
    pallas_call x1, Pallas kernels, per_device(): pl.pallas_call(functools.partial(kernel, n, n_sp, n_ep, chunk), out_shape...  144 us

profile of v4, /device:TPU:17, one launch (start us, length us, event | category | flops | bytes accessed | tf_op | source)
XLA Modules:
  0.0 145.7 jit_solution(12670831037107909375)
XLA Ops:
  0.0 143.6 %shard_map.73 = bf16[1024,2048]{1,0:T(8,128)(2,1)S(1)} custom-call(s32[8]{0:T(128)} %tenant_hbm.1, s32[8]{0:T(128)} %live_hbm.1, s32[32]{0:T(128)} %table_hbm.1, bf16[1024,2048]{1,0:T(8,128)(2,1)} %x_hbm.1, bf16[2048,8192]{1,0:T(8,128)(2,1)} %w_hbm.1, bf16[8,64,2048]{2,1,0:T(8,128)(2,1)} %bitcast.1, bf16[8,64,2048]{2,1,0:T(8,128)(2,1)} %b_hbm.1), custom_call_target="tpu_custom_call" | custom-call | tf_op jit(solution)/shard_map/pallas_call | solution.py:563
  143.6 2.0 %copy.9 = bf16[1024,2048]{1,0:T(8,128)(2,1)} copy(bf16[1024,2048]{1,0:T(8,128)(2,1)S(1)} %shard_map.73) | data formatting | bytes 8388608

commit v5 on v4

--- a/solution.py
+++ b/solution.py
@@ -9,7 +9,7 @@
 
 BLOCK = 128
 CHUNK = 512
-ENDS = 4
+ENDS = 8
 MESH = pl.DeviceIdType.MESH
 F32 = jnp.float32
 BF16 = jnp.bfloat16

time: 146 us -> 146 us (level)
  no operation moved by 1% of the time
where the time goes in v5:
time: 146 us
  Pallas kernels  144 us (99%)
  local copies, waits for them, and re-layouts  2.02 us (1%)
    pallas_call x1, Pallas kernels, per_device(): pl.pallas_call(functools.partial(kernel, n, n_sp, n_ep, chunk), out_shape...  144 us

profile of v5, /device:TPU:17, one launch (start us, length us, event | category | flops | bytes accessed | tf_op | source)
XLA Modules:
  0.0 145.8 jit_solution(7913272313803627099)
XLA Ops:
  0.0 143.7 %shard_map.73 = bf16[1024,2048]{1,0:T(8,128)(2,1)S(1)} custom-call(s32[8]{0:T(128)} %tenant_hbm.1, s32[8]{0:T(128)} %live_hbm.1, s32[32]{0:T(128)} %table_hbm.1, bf16[1024,2048]{1,0:T(8,128)(2,1)} %x_hbm.1, bf16[2048,8192]{1,0:T(8,128)(2,1)} %w_hbm.1, bf16[8,64,2048]{2,1,0:T(8,128)(2,1)} %bitcast.1, bf16[8,64,2048]{2,1,0:T(8,128)(2,1)} %b_hbm.1), custom_call_target="tpu_custom_call" | custom-call | tf_op jit(solution)/shard_map/pallas_call | solution.py:563
  143.7 2.0 %copy.9 = bf16[1024,2048]{1,0:T(8,128)(2,1)} copy(bf16[1024,2048]{1,0:T(8,128)(2,1)S(1)} %shard_map.73) | data formatting | bytes 8388608
